TPU v7x, 32 devices: a whole 2x2x4 slice. The times are simulated.
32 devices in a mesh: seq: 8 (over z, y), head: 4 (over x, core).
Axes of the slice: x: 2, y: 2, z: 4, core: 2. Of those that a mesh axis runs over, the one named last changes fastest.
Arguments:
- hidden_in: bfloat16 [2048, 2048], P('seq'), may hold values from -6 to 6
- attn_gain: float32 [2048], replicated, may hold values from 0.1 to 1.9
- w_qkv: bfloat16 [2048, 3, 2048], P(None, None, 'head'), may hold values from -0.125 to 0.125
- out_gain: float32 [2048], P('head'), may hold values from 0.1 to 1.9
- w_out: bfloat16 [2048, 2048], P('head'), may hold values from -0.125 to 0.125
- moe_gain: float32 [2048], replicated, may hold values from 0.1 to 1.9
- routes: int32 [2048, 8], P(('seq', 'head')), may hold values from 0 to 63, all different within a row; in each aligned block of 64 rows (0 to 63, 64 to 127, ...) at most 9 rows name the same one
- gate_weights: float32 [2048, 8], P(('seq', 'head')), may hold values from 0.1 to 0.6
- w_gate_up: bfloat16 [64, 2, 2048, 1024], P('seq', None, None, 'head'), may hold values from -0.125 to 0.125
- w_down: bfloat16 [64, 1024, 2048], P('seq', 'head'), may hold values from -0.1875 to 0.1875
Outputs:
- layer_out: bfloat16 [2048, 2048], P(('seq', 'head'))
Inputs may be any that keep to these rules, and one draw needn't show every extreme that they name: `routes`: each row names 8 different experts; within each aligned block of 64 rows (the rows of one device) no expert is named more than 9 times, a bound that some block reaches.
All inputs are finite; a program needn't handle non-finite values.
Results may differ from a plain program's by a relative error of at most 0.015.
Values may be sent and summed in bfloat16 or wider, within the bound.
A program may use at most 128 MiB of HBM per device.

v0:
```python
import jax
import jax.numpy as jnp
from jax import lax
from jax.sharding import PartitionSpec as P

D = 2048
DH = 128
EXPERTS = 64
TOP = 8


EPSILON = 1e-06


def rms_norm(values, gain):
    mean_square = jnp.mean(values * values, axis=-1, keepdims=True)
    return values * lax.rsqrt(mean_square + EPSILON) * gain


def slot_index(route_rows, capacity):
    flat_routes = route_rows.reshape(-1)
    experts_iota = jnp.arange(EXPERTS, dtype=jnp.int32)
    onehot = (flat_routes[:, None] == experts_iota[None, :]).astype(jnp.int32)
    before = jnp.cumsum(onehot, axis=0) - onehot
    position = jnp.sum(before * onehot, axis=1)
    return (flat_routes * capacity + position).reshape(route_rows.shape)


def expert_group(received, gate_up, down_rows):
    gate_val = jnp.einsum(
        "secd,edf->secf", received, gate_up[:, 0], preferred_element_type=jnp.float32
    )
    up_val = jnp.einsum(
        "secd,edf->secf", received, gate_up[:, 1], preferred_element_type=jnp.float32
    )
    hidden_units = (jax.nn.silu(gate_val) * up_val).astype(jnp.bfloat16)
    return jnp.einsum(
        "secf,efd->secd", hidden_units, down_rows, preferred_element_type=jnp.float32
    ).astype(jnp.bfloat16)


def on_device(
    hidden_in, attn_gain, w_qkv, out_gain, w_out, moe_gain, routes, gate_weights, w_gate_up, w_down
):
    token_count = hidden_in.shape[0]
    head_count = w_qkv.shape[2] // DH
    seq_size = lax.axis_size("seq")
    head_size = lax.axis_size("head")
    exp_local = w_gate_up.shape[0]
    resid_in = hidden_in.astype(jnp.float32)
    normed = rms_norm(resid_in, attn_gain).astype(jnp.bfloat16)
    projected = jnp.dot(
        normed, w_qkv.reshape(D, 3 * head_count * DH), preferred_element_type=jnp.float32
    )
    projected = projected.astype(jnp.bfloat16).reshape(token_count, 3, head_count, DH)
    query = projected[:, 0]
    keys_local = projected[:, 1]
    values_local = projected[:, 2]
    causal = jnp.tril(jnp.ones((token_count, token_count), jnp.float32))
    scores = (
        jnp.einsum("thd,shd->hts", query, keys_local, preferred_element_type=jnp.float32) * causal
    )
    local_part = jnp.einsum(
        "hts,shd->thd",
        scores.astype(jnp.bfloat16),
        values_local,
        preferred_element_type=jnp.float32,
    )
    own_state = jnp.einsum(
        "thd,the->hde", keys_local, values_local, preferred_element_type=jnp.float32
    )
    seq_index = lax.axis_index("seq")
    piece = lax.all_gather(own_state.astype(jnp.bfloat16), "seq", axis=0, tiled=True).astype(
        jnp.float32
    )
    shard_count = piece.shape[0] // head_count
    stacked = piece.reshape(shard_count, head_count, DH, DH)
    shard_ids = jnp.arange(shard_count, dtype=jnp.int32)
    keep = (shard_ids < seq_index)[:, None, None, None]
    earlier = jnp.zeros_like(own_state) + jnp.sum(jnp.where(keep, stacked, 0.0), axis=0)
    remote_part = jnp.einsum(
        "thd,hde->the", query.astype(jnp.float32), earlier, precision=lax.Precision.HIGHEST
    )
    attended = local_part + remote_part
    head_square = jnp.mean(attended * attended, axis=-1, keepdims=True)
    mixed = (attended * lax.rsqrt(head_square + EPSILON)).reshape(
        token_count, head_count * DH
    ) * out_gain
    mixed = mixed.astype(jnp.bfloat16)
    row_count = token_count // head_size
    attn_rows = lax.psum_scatter(
        jnp.dot(mixed, w_out, preferred_element_type=jnp.float32).astype(jnp.bfloat16),
        "head",
        scatter_dimension=0,
        tiled=True,
    ).astype(jnp.float32)
    resid = (
        lax.dynamic_slice_in_dim(resid_in, lax.axis_index("head") * row_count, row_count, 0)
        + attn_rows
    )
    normed2 = rms_norm(resid, moe_gain).astype(jnp.bfloat16)
    capacity = max(2, 9 * row_count * TOP // (8 * EXPERTS))
    slots = slot_index(routes, capacity)
    columns = jnp.arange(EXPERTS * capacity, dtype=jnp.int32)
    dispatch = jnp.sum((columns[:, None, None] == slots[None, :, :]).astype(jnp.bfloat16), axis=2)
    outgoing = jnp.dot(dispatch, normed2, preferred_element_type=jnp.float32).astype(jnp.bfloat16)
    outgoing = outgoing.reshape(seq_size, exp_local, capacity, D)
    copies = jnp.broadcast_to(outgoing[:, None], (seq_size, head_size, exp_local, capacity, D))
    copies = copies.reshape(seq_size * head_size, exp_local, capacity, D)
    partial_out = expert_group(
        lax.all_to_all(copies, ("seq", "head"), split_axis=0, concat_axis=0, tiled=True),
        w_gate_up,
        w_down,
    )
    returned = lax.all_to_all(partial_out, ("seq", "head"), split_axis=0, concat_axis=0, tiled=True)
    returned = returned.reshape(seq_size, head_size, exp_local, capacity, D).astype(jnp.float32)
    expert_out = jnp.sum(returned, axis=1).astype(jnp.bfloat16)
    flat_out = expert_out.reshape(EXPERTS * capacity, D)
    picked = jnp.take(flat_out, slots.reshape(-1), axis=0).reshape(row_count, TOP, D)
    moe_sum = jnp.sum(gate_weights[:, :, None] * picked.astype(jnp.float32), axis=1)
    return (resid + moe_sum).astype(jnp.bfloat16)


def solution(mesh):
    placed = (
        P("seq", None),
        P(),
        P(None, None, "head"),
        P("head"),
        P("head", None),
        P(),
        P(("seq", "head"), None),
        P(("seq", "head"), None),
        P("seq", None, None, "head"),
        P("seq", "head", None),
    )
    return jax.shard_map(
        on_device, mesh=mesh, in_specs=placed, out_specs=P(("seq", "head"), None), check_vma=False
    )
```

profile of v0, /device:TPU:0, one launch (start us, length us, event | category | flops | bytes accessed | tf_op | source)
XLA Modules:
  0.0 628.9 jit_solution(9571445138895907424)
XLA Ops:
  6.5 9.0 %copy.91 = bf16[2048,3,512]{0,2,1:T(8,128)(2,1)} copy(bf16[2048,3,512]{2,0,1:T(8,128)(2,1)} %param.12) | data formatting | bytes 12582912 | tf_op args[2]
  15.8 5.5 convolution_convert_fusion.2
  21.4 2.4 reshape.134
  23.8 2.2 fusion.45
  26.0 1.1 copy.121
  27.1 1.9 convolution_convert_fusion.3
  29.8 42.3 %all-gather.2.cloned.1.call-done = bf16[32,128,128]{2,1,0:T(8,128)(2,1)} async-done(((bf16[4,128,128]{2,1,0:T(8,128)(2,1)}), bf16[32,128,128]{2,1,0:T(8,128)(2,1)}) %all-gather.2.cloned.1.call-update) | async-done | bytes 1048592 | tf_op jit(solution)/shard_map/all_gather | solution.py:73
  72.1 1.5 fusion.16
  73.6 2.2 fusion.37
  75.8 2.6 multiply_reduce_fusion.3
  78.4 1.1 broadcast_multiply_fusion
  79.6 1.7 convolution_convert_fusion.1
  82.3 1.2 reduce-window.6
  84.6 20.5 %reduce-scatter.2.cloned.1.call-done = bf16[64,2048]{1,0:T(8,128)(2,1)} async-done(((bf16[256,2048]{1,0:T(8,128)(2,1)}), bf16[64,2048]{1,0:T(8,128)(2,1)}) %reduce-scatter.2.cloned.1.call-update) | async-done | bytes 262160 | tf_op jit(solution)/shard_map/reduce_scatter | solution.py:91
  105.2 1.1 multiply_reduce_fusion.2
  106.3 3.2 convolution_convert_fusion
  109.5 4.6 broadcast_in_dim.52
  114.1 3.7 copy.105
  117.8 5.1 broadcast_in_dim.53
  122.9 210.9 %all_to_all.10 = bf16[32,8,9,2048]{3,1,2,0:T(8,128)(2,1)} all-to-all(bf16[32,8,9,2048]{3,1,2,0:T(8,128)(2,1)} %bitcast.108), channel_id=1, replica_groups=mesh['seq'=8,'head'=4] {'seq','head'}, dimensions={0} | all-to-all | bytes 18874368 | tf_op jit(solution)/shard_map/all_to_all | solution.py:111
  333.8 13.0 %fusion.2 = f32[8,32,9,256]{3,1,2,0:T(8,128)} fusion(bf16[8,2,2048,256]{3,2,1,0:T(8,128)(2,1)} %param.18, bf16[32,8,9,2048]{3,1,2,0:T(8,128)(2,1)} %all_to_all.10), kind=kOutput, calls=%fused_computation.5 | convolution fusion | flops 2415919104 | bytes 20185088 | tf_op jit(solution)/shard_map/secd,edf->secf/dot_general | solution.py:30
  346.8 12.6 %fusion.12 = bf16[32,8,9,256]{3,0,2,1:T(8,128)(2,1)S(1)} fusion(f32[8,32,9,256]{3,1,2,0:T(8,128)} %fusion.2, bf16[8,2,2048,256]{3,2,1,0:T(8,128)(2,1)} %param.18, bf16[32,8,9,2048]{3,1,2,0:T(8,128)(2,1)} %all_to_all.10), kind=kOutput, calls=%fused_computation.18 | convolution fusion | flops 2419458048 | bytes 21364736 | tf_op jit(solution)/shard_map/secd,edf->secf/dot_general | solution.py:33
  359.3 8.6 %convert_bitcast_fusion = bf16[32,8,9,2048]{3,0,2,1:T(8,128)(2,1)} fusion(bf16[32,8,9,256]{3,0,2,1:T(8,128)(2,1)S(1)} %fusion.12, bf16[8,256,2048]{2,1,0:T(8,128)(2,1)} %param.19), kind=kOutput, calls=%fused_computation.2 | convolution fusion | flops 2420637696 | bytes 19005440 | tf_op jit(solution)/shard_map/secf,efd->secd/dot_general | solution.py:37
  368.0 12.5 %copy.110 = bf16[32,8,9,2048]{3,1,2,0:T(8,128)(2,1)} copy(bf16[32,8,9,2048]{3,0,2,1:T(8,128)(2,1)} %convert_bitcast_fusion) | data formatting | bytes 18874368 | tf_op jit(solution)/shard_map/convert_element_type | solution.py:39
  380.5 4.3 all-to-all-start.1
  385.2 208.7 %all-to-all-done.1 = bf16[32,8,9,2048]{3,1,2,0:T(8,128)(2,1)} async-done(((bf16[32,8,9,2048]{3,1,2,0:T(8,128)(2,1)}), bf16[32,8,9,2048]{3,1,2,0:T(8,128)(2,1)}, u32[]{:S(2)}, u32[]{:S(2)}) %all-to-all-start.1) | async-done | bytes 9437216 | tf_op jit(solution)/shard_map/all_to_all | solution.py:115
  593.9 6.1 bitcast_reduce_fusion
  600.0 3.6 copy.112
  603.6 4.7 reshape.142
  608.3 7.4 %gather_fusion = bf16[512,2048]{1,0:T(8,128)(2,1)} fusion(bf16[576,2048]{1,0:T(8,128)(2,1)} %reshape.142, s32[1024]{0:T(1024)S(1)} %pad_clamp_fusion), kind=kCustom, calls=%fused_computation | custom fusion | bytes 4196352 | tf_op jit(solution)/shard_map/jit(_take)/gather | solution.py:119
  615.7 4.0 multiply_reduce_fusion
  619.7 1.9 add_convert_fusion
  (52 shorter events, 3.7 us)
Async XLA Ops:
  6.5 73.1 %copy-start = (bf16[512,2048]{1,0:T(8,128)(2,1)S(1)}, bf16[512,2048]{1,0:T(8,128)(2,1)}, u32[]{:S(2)}) copy-start(bf16[512,2048]{1,0:T(8,128)(2,1)} %param.14) | copy-start | bytes 6291460
  6.5 9.0 %copy-start.3 = (bf16[256,2048]{1,0:T(8,128)(2,1)S(1)}, bf16[256,2048]{1,0:T(8,128)(2,1)}, u32[]{:S(2)}) copy-start(bf16[256,2048]{1,0:T(8,128)(2,1)} %param.10) | copy-start | bytes 3145732
  6.5 9.3 %copy-start.9 = (f32[2048]{0:T(1024)S(1)}, f32[2048]{0:T(1024)}, u32[]{:S(2)}) copy-start(f32[2048]{0:T(1024)} %param.11) | copy-start | bytes 24580
  6.5 65.5 %all-gather.2.cloned.1.call-start = ((), (), s32[]{:S(2)}) async-start(), calls=%async_computation.3 | async-start | bytes 1179648 | tf_op jit(solution)/shard_map/all_gather | solution.py:73
  29.0 76.2 %reduce-scatter.2.cloned.1.call-start = ((), (), s32[]{:S(2)}) async-start(), calls=%async_computation.4 | async-start | bytes 1310720 | tf_op jit(solution)/shard_map/reduce_scatter | solution.py:91
  73.6 5.8 copy-start.8
  81.3 0.7 copy-start.5
  81.3 25.0 %copy-start.6 = (f32[2048]{0:T(1024)S(1)}, f32[2048]{0:T(1024)}, u32[]{:S(2)}) copy-start(f32[2048]{0:T(1024)} %param.15) | copy-start | bytes 24580
  82.0 27.5 %copy-start.2 = (f32[256,2048]{1,0:T(8,128)}, f32[256,2048]{1,0:T(8,128)S(1)}, u32[]{:S(2)}) copy-start(f32[256,2048]{1,0:T(8,128)S(1)} %convert_element_type.61) | copy-start | bytes 6291460
  380.5 4.6 copy-start.7
  380.5 213.4 %all-to-all-start.1 = ((bf16[32,8,9,2048]{3,1,2,0:T(8,128)(2,1)}), bf16[32,8,9,2048]{3,1,2,0:T(8,128)(2,1)}, u32[]{:S(2)}, u32[]{:S(2)}) async-start(bf16[32,8,9,2048]{3,1,2,0:T(8,128)(2,1)} %copy.110), calls=%async_computation.2 | async-start | bytes 18874368 | tf_op jit(solution)/shard_map/all_to_all | solution.py:115
  608.3 13.3 %copy-start.1 = (bf16[512,2048]{1,0:T(8,128)(2,1)S(1)}, bf16[512,2048]{1,0:T(8,128)(2,1)}, u32[]{:S(2)}) copy-start(bf16[512,2048]{1,0:T(8,128)(2,1)} %param.14) | copy-start | bytes 6291460
  615.7 4.0 copy-start.4
Sparse Core Ops, SparseCore 0:
  29.1 42.9 all-gather.1
  81.5 23.6 reduce-scatter.1
where the time goes:
time: 637 us; the launch traced here: 629 us
  waiting for transfers between devices  272 us (43%)
  blocking collectives  211 us (33%)
  local copies, waits for them, and re-layouts  57.9 us (9%)
  matrix products  51.3 us (8%)
  other arithmetic  18.9 us (3%)
  between operations  14.1 us (2%)
    all_to_all x1, blocking collectives, on_device(): lax.all_to_all(copies, ('seq', 'head'), split_axis=0, concat_axis=0, tile...  211 us
    all_to_all x1, waiting for transfers between devices, on_device(): lax.all_to_all(partial_out, ('seq', 'head'), split_axis=0, concat_axis=0,...  209 us
    all_gather x1, waiting for transfers between devices, on_device(): lax.all_gather(own_state.astype(jnp.bfloat16), 'seq', axis=0, tiled=True)  42.3 us
    reduce_scatter x1, waiting for transfers between devices, on_device(): lax.psum_scatter(jnp.dot(mixed, w_out, preferred_element_type=jnp.float32...  20.5 us
    broadcast_in_dim x3, local copies, waits for them, and re-layouts, on_device(): jnp.broadcast_to(outgoing[:, None], (seq_size, head_size, exp_local, capa...  13.4 us
    dot_general x1, matrix products, expert_group(): jnp.einsum('secd,edf->secf', received, gate_up[:, 0], preferred_element_t...  13 us
  transfers between devices with their start and end apart: 3, of which 3 were waited for; matrix products, arithmetic and copies ran while one was open for 1% of the time, Pallas kernels for 0%

commit v1 on v0

v1 whole, which is shorter than its diff:
```python
import jax
import jax.numpy as jnp
from jax import lax
from jax.sharding import PartitionSpec as P

D = 2048
DH = 128
EXPERTS = 64
TOP = 8


EPSILON = 1e-06


def rms_norm(values, gain):
    mean_square = jnp.mean(values * values, axis=-1, keepdims=True)
    return values * lax.rsqrt(mean_square + EPSILON) * gain


def expert_tables(routes, gate_weights, exp_local, group_size, capacity):
    both = jnp.concatenate([routes.astype(jnp.float32), gate_weights], axis=1)
    both = lax.all_gather(both, ("seq", "head"), axis=0, tiled=True)
    groups = both.shape[0] // group_size
    expert_ids = lax.axis_index("seq") * exp_local + jnp.arange(exp_local, dtype=jnp.int32)
    match = both[:, None, :TOP] == expert_ids.astype(jnp.float32)[None, :, None]
    member = jnp.any(match, axis=2).reshape(groups, group_size, exp_local)
    weight = jnp.sum(jnp.where(match, both[:, None, TOP:], 0.0), axis=2)
    weight = weight.reshape(groups, group_size, exp_local)
    lower = jnp.tril(jnp.ones((group_size, group_size), jnp.bfloat16), -1)
    before = jnp.einsum(
        "ts,gsj->gjt", lower, member.astype(jnp.bfloat16), preferred_element_type=jnp.float32
    )
    member_t = jnp.transpose(member, (0, 2, 1))
    weight_t = jnp.transpose(weight, (0, 2, 1))
    places = jnp.arange(capacity, dtype=jnp.float32)
    picks = (before[:, :, None, :] == places[:, None]) & member_t[:, :, None, :]
    row_weight = jnp.sum(jnp.where(picks, weight_t[:, :, None, :], 0.0), axis=3)
    return picks.astype(jnp.bfloat16), row_weight


def on_device(
    hidden_in, attn_gain, w_qkv, out_gain, w_out, moe_gain, routes, gate_weights, w_gate_up, w_down
):
    token_count = hidden_in.shape[0]
    head_count = w_qkv.shape[2] // DH
    seq_size = lax.axis_size("seq")
    head_size = lax.axis_size("head")
    exp_local = w_gate_up.shape[0]
    row_count = token_count // head_size
    capacity = max(2, 9 * row_count * TOP // (8 * EXPERTS))
    blocks = 8
    group_size = blocks * row_count
    picks, row_weight = expert_tables(
        routes, gate_weights, exp_local, group_size, blocks * capacity
    )
    resid_in = hidden_in.astype(jnp.float32)
    normed = rms_norm(resid_in, attn_gain).astype(jnp.bfloat16)
    query, keys_local, values_local = (
        jnp.dot(normed, w_qkv[:, c], preferred_element_type=jnp.float32)
        .astype(jnp.bfloat16)
        .reshape(token_count, head_count, DH)
        for c in range(3)
    )
    causal = jnp.tril(jnp.ones((token_count, token_count), jnp.float32))
    scores = (
        jnp.einsum("thd,shd->hts", query, keys_local, preferred_element_type=jnp.float32) * causal
    )
    local_part = jnp.einsum(
        "hts,shd->thd",
        scores.astype(jnp.bfloat16),
        values_local,
        preferred_element_type=jnp.float32,
    )
    own_state = jnp.einsum(
        "thd,the->hde", keys_local, values_local, preferred_element_type=jnp.float32
    )
    seq_index = lax.axis_index("seq")
    piece = lax.all_gather(own_state.astype(jnp.bfloat16), "seq", axis=0, tiled=True).astype(
        jnp.float32
    )
    shard_count = piece.shape[0] // head_count
    stacked = piece.reshape(shard_count, head_count, DH, DH)
    shard_ids = jnp.arange(shard_count, dtype=jnp.int32)
    keep = (shard_ids < seq_index)[:, None, None, None]
    earlier = jnp.zeros_like(own_state) + jnp.sum(jnp.where(keep, stacked, 0.0), axis=0)
    remote_part = jnp.einsum(
        "thd,hde->the", query.astype(jnp.float32), earlier, precision=lax.Precision.HIGHEST
    )
    attended = local_part + remote_part
    head_square = jnp.mean(attended * attended, axis=-1, keepdims=True)
    mixed = (attended * lax.rsqrt(head_square + EPSILON)).reshape(
        token_count, head_count * DH
    ) * out_gain
    mixed = mixed.astype(jnp.bfloat16)
    attn_rows = lax.psum_scatter(
        jnp.dot(mixed, w_out, preferred_element_type=jnp.float32).astype(jnp.bfloat16),
        "head",
        scatter_dimension=0,
        tiled=True,
    ).astype(jnp.float32)
    resid = (
        lax.dynamic_slice_in_dim(resid_in, lax.axis_index("head") * row_count, row_count, 0)
        + attn_rows
    )
    normed2 = rms_norm(resid, moe_gain).astype(jnp.bfloat16)
    everyone = lax.all_gather(normed2, ("seq", "head"), axis=0, tiled=True)
    everyone = everyone.reshape(-1, group_size, D)
    rows_in = jnp.einsum(
        "gjct,gtd->jgcd", picks, everyone, preferred_element_type=jnp.float32
    ).astype(jnp.bfloat16)
    gate_val = jnp.einsum(
        "jgcd,jdf->jgcf", rows_in, w_gate_up[:, 0], preferred_element_type=jnp.float32
    )
    up_val = jnp.einsum(
        "jgcd,jdf->jgcf", rows_in, w_gate_up[:, 1], preferred_element_type=jnp.float32
    )
    weights = jnp.transpose(row_weight, (1, 0, 2))[..., None]
    hidden_units = (jax.nn.silu(gate_val) * up_val * weights).astype(jnp.bfloat16)
    rows_out = jnp.einsum(
        "jgcf,jfd->jgcd", hidden_units, w_down, preferred_element_type=jnp.float32
    ).astype(jnp.bfloat16)
    partial = jnp.einsum(
        "gjct,jgcd->gtd", picks, rows_out, preferred_element_type=jnp.float32
    ).astype(jnp.bfloat16)
    moe_sum = lax.psum_scatter(
        partial.reshape(-1, D), ("seq", "head"), scatter_dimension=0, tiled=True
    )
    return (resid + moe_sum.astype(jnp.float32)).astype(jnp.bfloat16)


def solution(mesh):
    placed = (
        P("seq", None),
        P(),
        P(None, None, "head"),
        P("head"),
        P("head", None),
        P(),
        P(("seq", "head"), None),
        P(("seq", "head"), None),
        P("seq", None, None, "head"),
        P("seq", "head", None),
    )
    return jax.shard_map(
        on_device, mesh=mesh, in_specs=placed, out_specs=P(("seq", "head"), None), check_vma=False
    )
```

time: 637 us -> 376 us (0.59); the launches traced: 629 us -> 375 us
  blocking collectives: 211 us -> 42 us
  local copies, waits for them, and re-layouts: 57.9 us -> 1.36 us
  waiting for transfers between devices: 272 us -> 244 us
  matrix products: 51.3 us -> 62.6 us
  other arithmetic: 18.9 us -> 11.8 us
    all_to_all x1 -> x0, blocking collectives: 211 us -> none  [on_device(): lax.all_to_all(copies, ('seq', 'head'), split_axis=0, concat_axis=0, tile...]
    all_to_all x1 -> x0, waiting for transfers between devices: 209 us -> none  [on_device(): lax.all_to_all(partial_out, ('seq', 'head'), split_axis=0, concat_axis=0,...]
    reduce_scatter x0 -> x1, waiting for transfers between devices: none -> 148 us  [on_device(): lax.psum_scatter(partial.reshape(-1, D), ('seq', 'head'), scatter_dimensi...]
    all_gather x0 -> x1, blocking collectives: none -> 42 us  [expert_tables(): both = lax.all_gather(both, ('seq', 'head'), axis=0, tiled=True)]
    all_gather x0 -> x1, waiting for transfers between devices: none -> 33.9 us  [on_device(): everyone = lax.all_gather(normed2, ('seq', 'head'), axis=0, tiled=True)]
    broadcast_in_dim x3 -> x0, local copies, waits for them, and re-layouts: 13.4 us -> none  [on_device(): jnp.broadcast_to(outgoing[:, None], (seq_size, head_size, exp_local, capa...]
    convert_element_type x1 -> x0, local copies, waits for them, and re-layouts: 12.5 us -> none  [expert_group(): return jnp.einsum('secf,efd->secd', hidden_units, down_rows, preferred_el...]
    dot_general x5 -> x8, matrix products: 42.9 us -> 54.3 us  [the longest x1 13.8 us: on_device(): jnp.einsum('gjct,jgcd->gtd', picks, rows_out, preferred_element_type=jnp....]
  transfers between devices with their start and end apart: 3 -> 4, of which waited for: 3 -> 4; matrix products, arithmetic and copies ran while one was open for 1% -> 2% of each run, Pallas kernels for 0% -> 0%
where the time goes in v1:
time: 376 us; the launch traced here: 375 us
  waiting for transfers between devices  244 us (65%)
  matrix products  62.6 us (17%)
  blocking collectives  42 us (11%)
  between operations  13.4 us (4%)
  other arithmetic  11.8 us (3%)
    reduce_scatter x1, waiting for transfers between devices, on_device(): lax.psum_scatter(partial.reshape(-1, D), ('seq', 'head'), scatter_dimensi...  148 us
    all_gather x1, blocking collectives, expert_tables(): both = lax.all_gather(both, ('seq', 'head'), axis=0, tiled=True)  42 us
    all_gather x1, waiting for transfers between devices, on_device(): lax.all_gather(own_state.astype(jnp.bfloat16), 'seq', axis=0, tiled=True)  39.2 us
    all_gather x1, waiting for transfers between devices, on_device(): everyone = lax.all_gather(normed2, ('seq', 'head'), axis=0, tiled=True)  33.9 us
    reduce_scatter x1, waiting for transfers between devices, on_device(): lax.psum_scatter(jnp.dot(mixed, w_out, preferred_element_type=jnp.float32...  23.5 us
    dot_general x1, matrix products, on_device(): jnp.einsum('gjct,jgcd->gtd', picks, rows_out, preferred_element_type=jnp....  13.8 us
    dot_general x1, matrix products, on_device(): jnp.einsum('gjct,gtd->jgcd', picks, everyone, preferred_element_type=jnp....  10.8 us
    dot_general x1, matrix products, on_device(): jnp.einsum('jgcd,jdf->jgcf', rows_in, w_gate_up[:, 0], preferred_element_...  10.1 us
  transfers between devices with their start and end apart: 4, of which 4 were waited for; matrix products, arithmetic and copies ran while one was open for 2% of the time, Pallas kernels for 0%

profile of v1, /device:TPU:0, one launch (start us, length us, event | category | flops | bytes accessed | tf_op | source)
XLA Modules:
  0.0 375.5 jit_solution(13111064960243815714)
XLA Ops:
  6.5 1.7 multiply_reduce_fusion
  8.2 3.5 fusion.60
  11.7 3.0 fusion.45
  14.8 1.1 copy.63
  15.9 1.8 convolution_convert_fusion.1
  17.8 0.7 fusion.78
  18.5 3.0 fusion.57
  21.5 39.2 %all-gather.4.cloned.1.call-done = bf16[32,128,128]{2,1,0:T(8,128)(2,1)} async-done(((bf16[4,128,128]{2,1,0:T(8,128)(2,1)}), bf16[32,128,128]{2,1,0:T(8,128)(2,1)}) %all-gather.4.cloned.1.call-update) | async-done | bytes 1048592 | tf_op jit(solution)/shard_map/all_gather | solution.py:78
  60.8 1.5 fusion.21
  62.3 2.2 fusion.70
  64.5 2.5 multiply_reduce_fusion.2
  67.0 1.1 broadcast_multiply_fusion
  68.1 0.1 fusion.66
  68.3 1.7 convolution_convert_fusion
  70.1 0.2 convert_element_type.68
  70.3 23.5 %reduce-scatter.3.cloned.1.call-done = bf16[64,2048]{1,0:T(8,128)(2,1)} async-done(((bf16[256,2048]{1,0:T(8,128)(2,1)}), bf16[64,2048]{1,0:T(8,128)(2,1)}) %reduce-scatter.3.cloned.1.call-update) | async-done | bytes 262160 | tf_op jit(solution)/shard_map/reduce_scatter | solution.py:95
  93.8 1.1 multiply_reduce_fusion.1
  95.0 1.8 multiply_convert_fusion.2
  96.9 42.0 %all-gather = f32[32,64,16]{1,2,0:T(8,128)S(1)} all-gather(f32[1,64,16]{1,2,0:T(8,128)S(1)} %maximum_bitcast_fusion), channel_id=1, replica_groups=mesh['seq'=8,'head'=4] {'seq','head'}, dimensions={0}, use_global_device_ids=true | all-gather | bytes 135168 | tf_op jit(solution)/shard_map/all_gather | solution.py:22
  138.9 0.1 copy.49
  139.0 0.1 reshape.93
  139.2 0.2 compare_reduce_fusion
  139.4 0.2 fusion.64
  139.6 0.3 fusion.68
  140.0 1.1 select_reduce_fusion
  141.1 33.9 %all-gather.6.cloned.1.call-done = bf16[2048,2048]{1,0:T(8,128)(2,1)} async-done(((bf16[64,2048]{1,0:T(8,128)(2,1)}), bf16[2048,2048]{1,0:T(8,128)(2,1)}) %all-gather.6.cloned.1.call-update) | async-done | bytes 8388624 | tf_op jit(solution)/shard_map/all_gather | solution.py:106
  175.0 10.8 %convert_bitcast_fusion = bf16[8,4,72,2048]{3,2,0,1:T(8,128)(2,1)} fusion(bf16[4,512,2048,1]{2,1,3,0:T(8,128)(2,1)} %bitcast.114, f32[4,8,512]{2,1,0:T(8,128)S(1)} %fusion.68, pred[4,8,512]{2,1,0:T(8,128)(4,1)S(1)} %bitcast.111), kind=kOutput, calls=%fused_computation.3 | convolution fusion | flops 4838916096 | bytes 17907712 | tf_op jit(solution)/shard_map/gjct,gtd->jgcd/dot_general | solution.py:108
  185.9 10.1 %fusion.4 = f32[8,4,72,256]{3,2,1,0:T(8,128)} fusion(bf16[8,2,2048,256]{3,2,1,0:T(8,128)(2,1)} %param.18, bf16[8,4,72,2048]{3,2,0,1:T(8,128)(2,1)} %convert_bitcast_fusion), kind=kOutput, calls=%fused_computation.6 | convolution fusion | flops 2415919104 | bytes 20185088 | tf_op jit(solution)/shard_map/jgcd,jdf->jgcf/dot_general | solution.py:111
  196.0 9.6 %multiply_convert_fusion = bf16[8,4,72,256]{3,2,1,0:T(8,128)(2,1)S(1)} fusion(f32[8,4,72,256]{3,2,1,0:T(8,128)} %fusion.4, bf16[8,2,2048,256]{3,2,1,0:T(8,128)(2,1)} %param.18, bf16[8,4,72,2048]{3,2,0,1:T(8,128)(2,1)} %convert_bitcast_fusion, f32[8,4,72]{2,1,0:T(4,128)S(1)} %copy.54), kind=kOutput, calls=%fused_computation.18 | convolution fusion | flops 2420047872 | bytes 21373952 | tf_op jit(solution)/shard_map/jgcd,jdf->jgcf/dot_general | solution.py:114
  205.6 13.8 %bitcast_convert_fusion = bf16[4,512,2048]{2,1,0:T(8,128)(2,1)} fusion(f32[4,8,512]{2,1,0:T(8,128)S(1)} %fusion.68, pred[4,8,512]{2,1,0:T(8,128)(4,1)S(1)} %bitcast.112, bf16[8,256,2048]{2,1,0:T(8,128)(2,1)} %param.19, bf16[8,4,72,256]{3,2,1,0:T(8,128)(2,1)S(1)} %multiply_convert_fusion), kind=kOutput, calls=%fused_computation | convolution fusion | flops 7259029504 | bytes 18038784 | tf_op jit(solution)/shard_map/gjct,jgcd->gtd/dot_general | solution.py:122
  219.5 147.6 %reduce-scatter.5.cloned.1.call-done = bf16[64,2048]{1,0:T(8,128)(2,1)} async-done(((bf16[2048,2048]{1,0:T(8,128)(2,1)}), bf16[64,2048]{1,0:T(8,128)(2,1)}) %reduce-scatter.5.cloned.1.call-update) | async-done | bytes 262160 | tf_op jit(solution)/shard_map/reduce_scatter | solution.py:125
  367.0 1.9 add_convert_fusion
  (38 shorter events, 0.3 us)
Async XLA Ops:
  6.5 61.7 %copy-start = (bf16[512,2048]{1,0:T(8,128)(2,1)S(1)}, bf16[512,2048]{1,0:T(8,128)(2,1)}, u32[]{:S(2)}) copy-start(bf16[512,2048]{1,0:T(8,128)(2,1)} %param.14) | copy-start | bytes 6291460
  6.5 54.2 %all-gather.4.cloned.1.call-start = ((), (), s32[]{:S(2)}) async-start(), calls=%async_computation.2 | async-start | bytes 1179648 | tf_op jit(solution)/shard_map/all_gather | solution.py:78
  8.2 3.5 copy-start.3
  8.2 3.5 copy-start.9
  17.7 76.1 %reduce-scatter.3.cloned.1.call-start = ((), (), s32[]{:S(2)}) async-start(), calls=%async_computation.3 | async-start | bytes 1310720 | tf_op jit(solution)/shard_map/reduce_scatter | solution.py:95
  62.3 5.8 %copy-start.8 = (f32[512]{0:T(512)S(1)}, f32[512]{0:T(512)}, u32[]{:S(2)}) copy-start(f32[512]{0:T(512)} %param.13) | copy-start | bytes 6148
  70.0 25.0 %copy-start.5 = (f32[2048]{0:T(1024)S(1)}, f32[2048]{0:T(1024)}, u32[]{:S(2)}) copy-start(f32[2048]{0:T(1024)} %param.15) | copy-start | bytes 24580
  70.0 26.8 %copy-start.6 = (s32[64,8]{0,1:T(8,128)S(1)}, s32[64,8]{0,1:T(8,128)}, u32[]{:S(2)}) copy-start(s32[64,8]{0,1:T(8,128)} %param.16) | copy-start | bytes 6148
  70.0 26.8 %copy-start.7 = (f32[64,8]{0,1:T(8,128)S(1)}, f32[64,8]{0,1:T(8,128)}, u32[]{:S(2)}) copy-start(f32[64,8]{0,1:T(8,128)} %param.17) | copy-start | bytes 6148
  70.0 105.0 %all-gather.6.cloned.1.call-start = ((), (), s32[]{:S(2)}) async-start(), calls=%async_computation.4 | async-start | bytes 8650752 | tf_op jit(solution)/shard_map/all_gather | solution.py:106
  70.3 69.6 %copy-start.2 = (f32[256,2048]{1,0:T(8,128)}, f32[256,2048]{1,0:T(8,128)S(1)}, u32[]{:S(2)}) copy-start(f32[256,2048]{1,0:T(8,128)S(1)} %convert_element_type.68) | copy-start | bytes 6291460
  96.8 270.3 %reduce-scatter.5.cloned.1.call-start = ((), (), s32[]{:S(2)}) async-start(), calls=%async_computation.5 | async-start | bytes 8650752 | tf_op jit(solution)/shard_map/reduce_scatter | solution.py:125
  219.4 147.6 %copy-start.4 = (bf16[64,2048]{1,0:T(8,128)(2,1)S(1)}, bf16[64,2048]{1,0:T(8,128)(2,1)}, u32[]{:S(2)}) copy-start(bf16[64,2048]{1,0:T(8,128)(2,1)} %reduce-scatter.3.cloned.1.call-done) | copy-start | bytes 786436
  219.5 149.5 %copy-start.1 = (bf16[512,2048]{1,0:T(8,128)(2,1)S(1)}, bf16[512,2048]{1,0:T(8,128)(2,1)}, u32[]{:S(2)}) copy-start(bf16[512,2048]{1,0:T(8,128)(2,1)} %param.14) | copy-start | bytes 6291460
Sparse Core Ops, SparseCore 0:
  17.8 42.9 all-gather.3
  70.1 23.6 reduce-scatter.2
  97.1 77.8 all-gather.5
  219.6 147.4 reduce-scatter.4

commit v2 on v1

--- a/solution.py
+++ b/solution.py
@@ -1,6 +1,9 @@
+import functools
 import jax
 import jax.numpy as jnp
 from jax import lax
+from jax.experimental import pallas as pl
+from jax.experimental.pallas import tpu as pltpu
 from jax.sharding import PartitionSpec as P
 
 D = 2048
@@ -17,9 +20,192 @@
     return values * lax.rsqrt(mean_square + EPSILON) * gain
 
 
+def axis_bits(name):
+    return [(name, bit) for bit in reversed(range(lax.axis_size(name).bit_length() - 1))]
+
+
+def own_bit(axis_and_bit):
+    name, bit = axis_and_bit
+    return (lax.axis_index(name) // (1 << bit)) % 2
+
+
+def partner(axis_and_bit):
+    name, bit = axis_and_bit
+    return {name: lax.axis_index(name) + (1 - 2 * own_bit(axis_and_bit)) * (1 << bit)}
+
+
+def greet(bits):
+    barrier = pltpu.get_barrier_semaphore()
+    for item in bits:
+        pl.semaphore_signal(
+            barrier, inc=1, device_id=partner(item), device_id_type=pl.DeviceIdType.MESH
+        )
+    pl.semaphore_wait(barrier, len(bits))
+
+
+def halving_orders(bits):
+    count = len(bits)
+    first = list(reversed(range(count)))
+    heads = [d for d in first if bits[d][0] == "head"]
+    others = [d for d in first if bits[d][0] != "head"]
+    if not heads or not others:
+        return [first, first]
+    return [first, heads[:1] + others[:1] + heads[1:] + others[1:]]
+
+
+def gather_kernel(bits, parts, x_ref, out_ref, send_sem, recv_sem, own_sem):
+    count = len(bits)
+    width = x_ref.shape[1] // parts
+    orders = [list(reversed(order)) for order in halving_orders(bits)]
+    mine = [own_bit(item) for item in bits]
+
+    def region(done, part):
+        index = tuple(slice(None) if d in done else mine[d] for d in range(count))
+        return out_ref.at[index + (slice(None), pl.ds(part * width, width))]
+
+    own = pltpu.make_async_copy(x_ref, out_ref.at[tuple(mine)], own_sem)
+    own.start()
+    greet(bits)
+    copies = [[None] * count for _ in range(parts)]
+    for stage in range(count):
+        for part in range(parts):
+            order = orders[part % 2]
+            if stage == 1 and part == 0:
+                own.wait()
+            if stage:
+                copies[part][stage - 1].wait_recv()
+            place = region(order[:stage], part)
+            source = x_ref.at[:, pl.ds(part * width, width)] if stage == 0 else place
+            copy = pltpu.make_async_remote_copy(
+                src_ref=source,
+                dst_ref=place,
+                send_sem=send_sem.at[part, stage],
+                recv_sem=recv_sem.at[part, stage],
+                device_id=partner(bits[order[stage]]),
+                device_id_type=pl.DeviceIdType.MESH,
+            )
+            copy.start()
+            copies[part][stage] = copy
+    for part in range(parts):
+        copies[part][count - 1].wait_recv()
+    for part in range(parts):
+        for stage in range(count):
+            copies[part][stage].wait_send()
+
+
+def gather(x, bits, parts, collective_id):
+    count = len(bits)
+    rows, columns = x.shape
+    out = pl.pallas_call(
+        functools.partial(gather_kernel, bits, parts),
+        out_shape=jax.ShapeDtypeStruct((2,) * count + x.shape, x.dtype),
+        in_specs=[pl.BlockSpec(memory_space=pl.ANY)],
+        out_specs=pl.BlockSpec(memory_space=pl.ANY),
+        scratch_shapes=[
+            pltpu.SemaphoreType.DMA((parts, count)),
+            pltpu.SemaphoreType.DMA((parts, count)),
+            pltpu.SemaphoreType.DMA,
+        ],
+        compiler_params=pltpu.CompilerParams(collective_id=collective_id, has_side_effects=True),
+        name=f"gather{collective_id}",
+    )(x)
+    return out.reshape((1 << count) * rows, columns)
+
+
+def reduce_kernel(bits, parts, x_ref, out_ref, keep, *rest):
+    count = len(bits)
+    received, (send_sem, recv_sem, own_sem) = rest[:count], rest[count:]
+    width = x_ref.shape[-1] // parts
+    orders = halving_orders(bits)
+    mine = [own_bit(item) for item in bits]
+
+    def columns(part):
+        return (slice(None), pl.ds(part * width, width))
+
+    def kept(done, part, flip=None):
+        return tuple(
+            (1 - mine[d]) if d == flip else (mine[d] if d in done else slice(None))
+            for d in range(count - 1)
+        ) + columns(part)
+
+    whole = (slice(None),) * (count - 1)
+    own = []
+    for part in range(parts):
+        copy = pltpu.make_async_copy(
+            x_ref.at[whole + (mine[-1],) + columns(part)],
+            keep.at[whole + columns(part)],
+            own_sem.at[part],
+        )
+        copy.start()
+        own.append(copy)
+    greet(bits)
+    copies = [[None] * count for _ in range(parts)]
+    for stage in range(count + 1):
+        for part in range(parts):
+            order = orders[part % 2]
+            if stage:
+                if stage == 1:
+                    own[part].wait()
+                copies[part][stage - 1].wait_recv()
+                place = kept(order[:stage], part)
+                piece = (slice(None),) * (count - stage) + columns(part)
+                total = keep[place] + received[stage - 1][piece]
+                if stage == count:
+                    out_ref[:, pl.ds(part * width, width)] = total
+                    continue
+                keep[place] = total
+            if stage == 0:
+                source = x_ref.at[whole + (1 - mine[-1],) + columns(part)]
+            else:
+                source = keep.at[kept(order[:stage], part, order[stage])]
+            landing = (slice(None),) * (count - 1 - stage) + columns(part)
+            copy = pltpu.make_async_remote_copy(
+                src_ref=source,
+                dst_ref=received[stage].at[landing],
+                send_sem=send_sem.at[part, stage],
+                recv_sem=recv_sem.at[part, stage],
+                device_id=partner(bits[order[stage]]),
+                device_id_type=pl.DeviceIdType.MESH,
+            )
+            copy.start()
+            copies[part][stage] = copy
+    for part in range(parts):
+        for stage in range(count):
+            copies[part][stage].wait_send()
+
+
+def reduce_scatter(x, bits, parts, collective_id):
+    count = len(bits)
+    rows, columns = x.shape[0] >> count, x.shape[1]
+    block = (rows, columns)
+    return pl.pallas_call(
+        functools.partial(reduce_kernel, bits, parts),
+        out_shape=jax.ShapeDtypeStruct(block, x.dtype),
+        in_specs=[pl.BlockSpec(memory_space=pl.ANY)],
+        out_specs=pl.BlockSpec(memory_space=pltpu.VMEM),
+        scratch_shapes=[pltpu.VMEM((2,) * (count - 1) + block, x.dtype)]
+        + [pltpu.VMEM((2,) * (count - 1 - stage) + block, x.dtype) for stage in range(count)]
+        + [
+            pltpu.SemaphoreType.DMA((parts, count)),
+            pltpu.SemaphoreType.DMA((parts, count)),
+            pltpu.SemaphoreType.DMA((parts,)),
+        ],
+        compiler_params=pltpu.CompilerParams(
+            collective_id=collective_id,
+            has_side_effects=True,
+            vmem_limit_bytes=(3 * x.shape[0] * columns + 16 * rows * columns) + (4 << 20),
+        ),
+        name=f"reduce{collective_id}",
+    )(x.reshape((2,) * count + block))
+
+
 def expert_tables(routes, gate_weights, exp_local, group_size, capacity):
     both = jnp.concatenate([routes.astype(jnp.float32), gate_weights], axis=1)
-    both = lax.all_gather(both, ("seq", "head"), axis=0, tiled=True)
+    rows = both.shape[0]
+    both = jnp.pad(both.T, ((0, 0), (0, -rows % 128)))
+    both = gather(both, axis_bits("seq") + axis_bits("head"), 1, 0)
+    both = jnp.transpose(both.reshape(-1, 2 * TOP, both.shape[1])[:, :, :rows], (0, 2, 1))
+    both = both.reshape(-1, 2 * TOP)
     groups = both.shape[0] // group_size
     expert_ids = lax.axis_index("seq") * exp_local + jnp.arange(exp_local, dtype=jnp.int32)
     match = both[:, None, :TOP] == expert_ids.astype(jnp.float32)[None, :, None]
@@ -75,9 +261,10 @@
         "thd,the->hde", keys_local, values_local, preferred_element_type=jnp.float32
     )
     seq_index = lax.axis_index("seq")
-    piece = lax.all_gather(own_state.astype(jnp.bfloat16), "seq", axis=0, tiled=True).astype(
-        jnp.float32
-    )
+    piece = gather(
+        own_state.astype(jnp.bfloat16).reshape(head_count * DH, DH), axis_bits("seq"), 1, 1
+    )
+    piece = piece.reshape(-1, DH, DH).astype(jnp.float32)
     shard_count = piece.shape[0] // head_count
     stacked = piece.reshape(shard_count, head_count, DH, DH)
     shard_ids = jnp.arange(shard_count, dtype=jnp.int32)
@@ -92,18 +279,18 @@
         token_count, head_count * DH
     ) * out_gain
     mixed = mixed.astype(jnp.bfloat16)
-    attn_rows = lax.psum_scatter(
+    attn_rows = reduce_scatter(
         jnp.dot(mixed, w_out, preferred_element_type=jnp.float32).astype(jnp.bfloat16),
-        "head",
-        scatter_dimension=0,
-        tiled=True,
+        axis_bits("head"),
+        2,
+        2,
     ).astype(jnp.float32)
     resid = (
         lax.dynamic_slice_in_dim(resid_in, lax.axis_index("head") * row_count, row_count, 0)
         + attn_rows
     )
     normed2 = rms_norm(resid, moe_gain).astype(jnp.bfloat16)
-    everyone = lax.all_gather(normed2, ("seq", "head"), axis=0, tiled=True)
+    everyone = gather(normed2, axis_bits("seq") + axis_bits("head"), 4, 3)
     everyone = everyone.reshape(-1, group_size, D)
     rows_in = jnp.einsum(
         "gjct,gtd->jgcd", picks, everyone, preferred_element_type=jnp.float32
@@ -122,8 +309,8 @@
     partial = jnp.einsum(
         "gjct,jgcd->gtd", picks, rows_out, preferred_element_type=jnp.float32
     ).astype(jnp.bfloat16)
-    moe_sum = lax.psum_scatter(
-        partial.reshape(-1, D), ("seq", "head"), scatter_dimension=0, tiled=True
+    moe_sum = reduce_scatter(
+        partial.reshape(-1, D), axis_bits("seq") + axis_bits("head"), 4, 4
     )
     return (resid + moe_sum.astype(jnp.float32)).astype(jnp.bfloat16)
 

time: 376 us -> 254 us (0.68)
  waiting for transfers between devices: 244 us -> 0 us
  Pallas kernels: 0 us -> 178 us
  blocking collectives: 42 us -> 0 us
  between operations: 13.4 us -> 0.22 us
  matrix products: 62.6 us -> 57.4 us
  local copies, waits for them, and re-layouts: 1.36 us -> 6.28 us
    pallas_call x0 -> x5, Pallas kernels: none -> 178 us  [the longest x3 111 us: gather(): pl.pallas_call(functools.partial(gather_kernel, bits, parts), out_shape=j...]
    reduce_scatter x2 -> x0, waiting for transfers between devices: 171 us -> none  [the longest x1 148 us: on_device(): lax.psum_scatter(partial.reshape(-1, D), ('seq', 'head'), scatter_dimensi...]
    all_gather x2 -> x0, waiting for transfers between devices: 73.2 us -> none  [the longest x1 39.2 us: on_device(): lax.all_gather(own_state.astype(jnp.bfloat16), 'seq', axis=0, tiled=True)]
    all_gather x1 -> x0, blocking collectives: 42 us -> none  [expert_tables(): both = lax.all_gather(both, ('seq', 'head'), axis=0, tiled=True)]
    unnamed x21 -> x19, local copies, waits for them, and re-layouts: 0.18 us -> 4.46 us
  transfers between devices with their start and end apart: 4 -> 0, of which waited for: 4 -> 0; matrix products, arithmetic and copies ran while one was open for 2% -> 0% of each run, Pallas kernels for 0% -> 0%
where the time goes in v2:
time: 254 us; the launch traced here: 253 us
  Pallas kernels  178 us (70%)
  matrix products  57.4 us (23%)
  other arithmetic  11.5 us (5%)
  local copies, waits for them, and re-layouts  6.28 us (2%)
    pallas_call x3, Pallas kernels, gather(): pl.pallas_call(functools.partial(gather_kernel, bits, parts), out_shape=j...  111 us
    pallas_call x2, Pallas kernels, reduce_scatter(): pl.pallas_call(functools.partial(reduce_kernel, bits, parts), out_shape=j...  67.2 us
    dot_general x1, matrix products, on_device(): jnp.einsum('gjct,jgcd->gtd', picks, rows_out, preferred_element_type=jnp....  14 us
    dot_general x1, matrix products, on_device(): jnp.einsum('gjct,gtd->jgcd', picks, everyone, preferred_element_type=jnp....  10.8 us
    dot_general x1, matrix products, on_device(): jnp.einsum('jgcd,jdf->jgcf', rows_in, w_gate_up[:, 1], preferred_element_...  9.98 us
    dot_general x1, matrix products, on_device(): jnp.einsum('jgcd,jdf->jgcf', rows_in, w_gate_up[:, 0], preferred_element_...  8.69 us
    dot_general x3, matrix products, on_device(): jnp.dot(normed, w_qkv[:, c], preferred_element_type=jnp.float32)  6.39 us

profile of v2, /device:TPU:0, one launch (start us, length us, event | category | flops | bytes accessed | tf_op | source)
XLA Modules:
  0.0 253.4 jit_solution(13928739304364409414)
XLA Ops:
  0.0 1.7 multiply_reduce_fusion
  1.7 0.7 convert_element_type.85
  2.4 0.7 maximum_bitcast_fusion
  3.1 0.6 pad.4.x_ref
  3.7 19.3 %gather0.1 = f32[2,2,2,2,2,16,128]{6,5,4,3,2,1,0:T(8,128)} custom-call(f32[16,128]{1,0:T(8,128)} %pad.4.x_ref), custom_call_target="tpu_custom_call" | custom-call | tf_op jit(solution)/shard_map/gather0/pallas_call | solution.py:99
  23.0 1.0 copy.102
  24.4 0.2 compare_reduce_fusion
  24.7 0.3 fusion.67
  25.0 1.1 select_reduce_fusion
  26.2 3.4 %fusion.56 = bf16[32,4,8,128]{3,2,1,0:T(8,128)(2,1)} fusion(bf16[2048,3,512]{2,0,1:T(8,128)(2,1)} %param.12, f32[2048]{0:T(1024)} %param.11, f32[256]{0:T(256)S(1)} %add_rsqrt_fusion.1, bf16[256,2048]{1,0:T(8,128)(2,1)S(1)} %copy-done.4), kind=kOutput, calls=%fused_computation.44 | convolution fusion | flops 539099136 | bytes 3417088 | tf_op jit(solution)/shard_map/dot_general | solution.py:245
  29.6 1.5 fusion.59
  31.1 1.5 fusion.44
  32.6 1.1 copy.65
  33.7 1.8 convolution_convert_fusion.1
  35.5 0.7 fusion.77
  36.2 29.3 %gather1.1 = bf16[2,2,2,512,128]{4,3,2,1,0:T(8,128)(2,1)} custom-call(bf16[512,128]{1,0:T(8,128)(2,1)} %bitcast.118), custom_call_target="tpu_custom_call" | custom-call | tf_op jit(solution)/shard_map/gather1/pallas_call | solution.py:99
  65.5 1.5 select_reduce_fusion.1
  67.1 2.2 fusion.69
  69.2 2.5 multiply_reduce_fusion.2
  71.8 1.1 broadcast_multiply_fusion
  73.0 0.7 convolution_convert_fusion
  73.8 9.2 %reduce2.1 = bf16[64,2048]{1,0:T(8,128)(2,1)S(1)} custom-call(bf16[2,2,64,2048]{3,2,1,0:T(8,128)(2,1)S(1)} %bitcast.111), custom_call_target="tpu_custom_call" | custom-call | tf_op jit(solution)/shard_map/reduce2/pallas_call | solution.py:181
  83.0 0.2 convert_element_type.74
  83.5 1.1 multiply_convert_fusion.2.x_ref
  84.6 62.1 %gather3.1 = bf16[2,2,2,2,2,64,2048]{6,5,4,3,2,1,0:T(8,128)(2,1)} custom-call(bf16[64,2048]{1,0:T(8,128)(2,1)} %multiply_convert_fusion.2.x_ref), custom_call_target="tpu_custom_call" | custom-call | tf_op jit(solution)/shard_map/gather3/pallas_call | solution.py:99
  146.7 10.8 %convert_bitcast_fusion = bf16[8,4,72,2048]{3,2,0,1:T(8,128)(2,1)} fusion(bf16[4,512,2048,1]{2,1,3,0:T(8,128)(2,1)} %bitcast.112, f32[4,8,512]{2,1,0:T(8,128)S(1)} %fusion.67, pred[4,8,512]{2,1,0:T(8,128)(4,1)S(1)} %bitcast.122), kind=kOutput, calls=%fused_computation.3 | convolution fusion | flops 4838916096 | bytes 17907712 | tf_op jit(solution)/shard_map/gjct,gtd->jgcd/dot_general | solution.py:295
  157.6 8.7 %fusion.4 = f32[8,4,72,256]{3,2,1,0:T(8,128)S(1)} fusion(bf16[8,2,2048,256]{3,2,1,0:T(8,128)(2,1)} %param.18, bf16[8,4,72,2048]{3,2,0,1:T(8,128)(2,1)} %convert_bitcast_fusion), kind=kOutput, calls=%fused_computation.6 | convolution fusion | flops 2415919104 | bytes 20185088 | tf_op jit(solution)/shard_map/jgcd,jdf->jgcf/dot_general | solution.py:298
  166.3 10.0 %multiply_convert_fusion = bf16[8,4,72,256]{3,2,1,0:T(8,128)(2,1)} fusion(f32[8,4,72,256]{3,2,1,0:T(8,128)S(1)} %fusion.4, bf16[8,2,2048,256]{3,2,1,0:T(8,128)(2,1)} %param.18, bf16[8,4,72,2048]{3,2,0,1:T(8,128)(2,1)} %convert_bitcast_fusion, f32[8,4,72]{2,1,0:T(4,128)S(1)} %copy.55), kind=kOutput, calls=%fused_computation.18 | convolution fusion | flops 2420047872 | bytes 21373952 | tf_op jit(solution)/shard_map/jgcd,jdf->jgcf/dot_general | solution.py:301
  176.3 14.0 %bitcast_convert_fusion = bf16[4,512,2048]{2,1,0:T(8,128)(2,1)} fusion(f32[4,8,512]{2,1,0:T(8,128)S(1)} %fusion.67, pred[4,8,512]{2,1,0:T(8,128)(4,1)S(1)} %bitcast.123, bf16[8,256,2048]{2,1,0:T(8,128)(2,1)} %param.19, bf16[8,4,72,256]{3,2,1,0:T(8,128)(2,1)} %multiply_convert_fusion), kind=kOutput, calls=%fused_computation | convolution fusion | flops 7259029504 | bytes 18038784 | tf_op jit(solution)/shard_map/gjct,jgcd->gtd/dot_general | solution.py:309
  190.2 3.4 %copy-done.2 = bf16[4,512,2048]{2,1,0:T(8,128)(2,1)S(1)} copy-done((bf16[4,512,2048]{2,1,0:T(8,128)(2,1)S(1)}, bf16[4,512,2048]{2,1,0:T(8,128)(2,1)}, u32[]{:S(2)}) %copy-start.2) | copy-done | bytes 8388632
  193.6 57.9 %reduce4.1 = bf16[64,2048]{1,0:T(8,128)(2,1)S(1)} custom-call(bf16[2,2,2,2,2,64,2048]{6,5,4,3,2,1,0:T(8,128)(2,1)S(1)} %bitcast.110), custom_call_target="tpu_custom_call" | custom-call | tf_op jit(solution)/shard_map/reduce4/pallas_call | solution.py:181
  251.5 1.8 add_convert_fusion
  (29 shorter events, 0.8 us)
Async XLA Ops:
  0.0 73.0 %copy-start = (bf16[512,2048]{1,0:T(8,128)(2,1)S(1)}, bf16[512,2048]{1,0:T(8,128)(2,1)}, u32[]{:S(2)}) copy-start(bf16[512,2048]{1,0:T(8,128)(2,1)} %param.14) | copy-start | bytes 6291460
  0.0 26.2 %copy-start.4 = (bf16[256,2048]{1,0:T(8,128)(2,1)S(1)}, bf16[256,2048]{1,0:T(8,128)(2,1)}, u32[]{:S(2)}) copy-start(bf16[256,2048]{1,0:T(8,128)(2,1)} %param.10) | copy-start | bytes 3145732
  24.7 4.9 %copy-start.7 = (bf16[2048,3,512]{2,0,1:T(8,128)(2,1)S(1)}, bf16[2048,3,512]{2,0,1:T(8,128)(2,1)}, u32[]{:S(2)}) copy-start(bf16[2048,3,512]{2,0,1:T(8,128)(2,1)} %param.12) | copy-start | bytes 18874372
  26.2 3.4 %copy-start.8 = (f32[2048]{0:T(1024)S(1)}, f32[2048]{0:T(1024)}, u32[]{:S(2)}) copy-start(f32[2048]{0:T(1024)} %param.11) | copy-start | bytes 24580
  67.0 5.8 %copy-start.6 = (f32[512]{0:T(512)S(1)}, f32[512]{0:T(512)}, u32[]{:S(2)}) copy-start(f32[512]{0:T(512)} %param.13) | copy-start | bytes 6148
  73.8 9.7 %copy-start.5 = (f32[2048]{0:T(1024)S(1)}, f32[2048]{0:T(1024)}, u32[]{:S(2)}) copy-start(f32[2048]{0:T(1024)} %param.15) | copy-start | bytes 24580
  83.3 63.5 %copy-start.3 = (f32[256,2048]{1,0:T(8,128)}, f32[256,2048]{1,0:T(8,128)S(1)}, u32[]{:S(2)}) copy-start(f32[256,2048]{1,0:T(8,128)S(1)} %convert_element_type.74) | copy-start | bytes 6291460
  190.2 3.4 %copy-start.2 = (bf16[4,512,2048]{2,1,0:T(8,128)(2,1)S(1)}, bf16[4,512,2048]{2,1,0:T(8,128)(2,1)}, u32[]{:S(2)}) copy-start(bf16[4,512,2048]{2,1,0:T(8,128)(2,1)} %bitcast_convert_fusion) | copy-start | bytes 25165828
  193.6 59.8 %copy-start.1 = (bf16[512,2048]{1,0:T(8,128)(2,1)S(1)}, bf16[512,2048]{1,0:T(8,128)(2,1)}, u32[]{:S(2)}) copy-start(bf16[512,2048]{1,0:T(8,128)(2,1)} %param.14) | copy-start | bytes 6291460

commit v3 on v2

--- a/solution.py
+++ b/solution.py
@@ -41,6 +41,84 @@
             barrier, inc=1, device_id=partner(item), device_id_type=pl.DeviceIdType.MESH
         )
     pl.semaphore_wait(barrier, len(bits))
+
+
+def early_kernel(bits, scan_bits, x_ref, state_ref, out_ref, earlier_ref, *scratch):
+    everyone, total, sent, landed, send_sem, recv_sem, scan_send, scan_recv, own_sem = scratch
+    count = len(bits)
+    mine = [own_bit(item) for item in bits]
+    own = pltpu.make_async_copy(x_ref, everyone.at[tuple(mine)], own_sem)
+    own.start()
+    total[...] = state_ref[...]
+    earlier_ref[...] = jnp.zeros_like(earlier_ref)
+    greet(bits)
+    own.wait()
+    copies = []
+    for stage in range(count):
+        dim = count - 1 - stage
+        place = everyone.at[tuple(mine[: dim + 1])]
+        copy = pltpu.make_async_remote_copy(
+            src_ref=place,
+            dst_ref=place,
+            send_sem=send_sem.at[stage],
+            recv_sem=recv_sem.at[stage],
+            device_id=partner(bits[dim]),
+            device_id_type=pl.DeviceIdType.MESH,
+        )
+        copy.start()
+        copies.append(copy)
+        scan = None
+        if stage < len(scan_bits):
+            item = scan_bits[len(scan_bits) - 1 - stage]
+            sent[stage] = total[...].astype(sent.dtype)
+            scan = pltpu.make_async_remote_copy(
+                src_ref=sent.at[stage],
+                dst_ref=landed.at[stage],
+                send_sem=scan_send.at[stage],
+                recv_sem=scan_recv.at[stage],
+                device_id=partner(item),
+                device_id_type=pl.DeviceIdType.MESH,
+            )
+            scan.start()
+            copies.append(scan)
+        copy.wait_recv()
+        if scan is not None:
+            scan.wait_recv()
+            other = landed[stage].astype(jnp.float32)
+            total[...] += other
+            earlier_ref[...] += other * own_bit(item).astype(jnp.float32)
+    out_ref[...] = everyone[...]
+    for copy in copies:
+        copy.wait_send()
+
+
+def early_exchange(x, state, bits, scan_bits, collective_id):
+    count, steps = len(bits), len(scan_bits)
+    gathered, earlier = pl.pallas_call(
+        functools.partial(early_kernel, bits, scan_bits),
+        out_shape=[
+            jax.ShapeDtypeStruct((2,) * count + x.shape, x.dtype),
+            jax.ShapeDtypeStruct(state.shape, jnp.float32),
+        ],
+        in_specs=[pl.BlockSpec(memory_space=pltpu.VMEM)] * 2,
+        out_specs=[pl.BlockSpec(memory_space=pltpu.VMEM)] * 2,
+        scratch_shapes=[
+            pltpu.VMEM((2,) * count + x.shape, x.dtype),
+            pltpu.VMEM(state.shape, jnp.float32),
+            pltpu.VMEM((steps,) + state.shape, jnp.bfloat16),
+            pltpu.VMEM((steps,) + state.shape, jnp.bfloat16),
+            pltpu.SemaphoreType.DMA((count,)),
+            pltpu.SemaphoreType.DMA((count,)),
+            pltpu.SemaphoreType.DMA((steps,)),
+            pltpu.SemaphoreType.DMA((steps,)),
+            pltpu.SemaphoreType.DMA,
+        ],
+        compiler_params=pltpu.CompilerParams(
+            collective_id=collective_id, has_side_effects=True, vmem_limit_bytes=24 << 20
+        ),
+        name=f"early{collective_id}",
+    )(x, state)
+    return gathered, earlier
 
 
 def halving_orders(bits):
@@ -199,12 +277,8 @@
     )(x.reshape((2,) * count + block))
 
 
-def expert_tables(routes, gate_weights, exp_local, group_size, capacity):
-    both = jnp.concatenate([routes.astype(jnp.float32), gate_weights], axis=1)
-    rows = both.shape[0]
-    both = jnp.pad(both.T, ((0, 0), (0, -rows % 128)))
-    both = gather(both, axis_bits("seq") + axis_bits("head"), 1, 0)
-    both = jnp.transpose(both.reshape(-1, 2 * TOP, both.shape[1])[:, :, :rows], (0, 2, 1))
+def expert_tables(both, rows, exp_local, group_size, capacity):
+    both = jnp.transpose(both.reshape(-1, 2 * TOP, both.shape[-1])[:, :, :rows], (0, 2, 1))
     both = both.reshape(-1, 2 * TOP)
     groups = both.shape[0] // group_size
     expert_ids = lax.axis_index("seq") * exp_local + jnp.arange(exp_local, dtype=jnp.int32)
@@ -236,9 +310,6 @@
     capacity = max(2, 9 * row_count * TOP // (8 * EXPERTS))
     blocks = 8
     group_size = blocks * row_count
-    picks, row_weight = expert_tables(
-        routes, gate_weights, exp_local, group_size, blocks * capacity
-    )
     resid_in = hidden_in.astype(jnp.float32)
     normed = rms_norm(resid_in, attn_gain).astype(jnp.bfloat16)
     query, keys_local, values_local = (
@@ -260,16 +331,18 @@
     own_state = jnp.einsum(
         "thd,the->hde", keys_local, values_local, preferred_element_type=jnp.float32
     )
-    seq_index = lax.axis_index("seq")
-    piece = gather(
-        own_state.astype(jnp.bfloat16).reshape(head_count * DH, DH), axis_bits("seq"), 1, 1
-    )
-    piece = piece.reshape(-1, DH, DH).astype(jnp.float32)
-    shard_count = piece.shape[0] // head_count
-    stacked = piece.reshape(shard_count, head_count, DH, DH)
-    shard_ids = jnp.arange(shard_count, dtype=jnp.int32)
-    keep = (shard_ids < seq_index)[:, None, None, None]
-    earlier = jnp.zeros_like(own_state) + jnp.sum(jnp.where(keep, stacked, 0.0), axis=0)
+    both = jnp.concatenate([routes.astype(jnp.float32), gate_weights], axis=1)
+    both, earlier = early_exchange(
+        jnp.pad(both.T, ((0, 0), (0, -row_count % 128))),
+        own_state.reshape(head_count * DH, DH),
+        axis_bits("seq") + axis_bits("head"),
+        axis_bits("seq"),
+        0,
+    )
+    earlier = earlier.reshape(own_state.shape)
+    picks, row_weight = expert_tables(
+        both, row_count, exp_local, group_size, blocks * capacity
+    )
     remote_part = jnp.einsum(
         "thd,hde->the", query.astype(jnp.float32), earlier, precision=lax.Precision.HIGHEST
     )
@@ -290,7 +363,7 @@
         + attn_rows
     )
     normed2 = rms_norm(resid, moe_gain).astype(jnp.bfloat16)
-    everyone = gather(normed2, axis_bits("seq") + axis_bits("head"), 4, 3)
+    everyone = gather(normed2, axis_bits("seq") + axis_bits("head"), 8, 3)
     everyone = everyone.reshape(-1, group_size, D)
     rows_in = jnp.einsum(
         "gjct,gtd->jgcd", picks, everyone, preferred_element_type=jnp.float32
@@ -310,7 +383,7 @@
         "gjct,jgcd->gtd", picks, rows_out, preferred_element_type=jnp.float32
     ).astype(jnp.bfloat16)
     moe_sum = reduce_scatter(
-        partial.reshape(-1, D), axis_bits("seq") + axis_bits("head"), 4, 4
+        partial.reshape(-1, D), axis_bits("seq") + axis_bits("head"), 8, 4
     )
     return (resid + moe_sum.astype(jnp.float32)).astype(jnp.bfloat16)
 

time: 254 us -> 226 us (0.89)
  Pallas kernels: 178 us -> 149 us
  matrix products: 57.4 us -> 60.8 us
    pallas_call x3 -> x1, Pallas kernels: 111 us -> 56.8 us  [gather(): pl.pallas_call(functools.partial(gather_kernel, bits, parts), out_shape=j...]
    pallas_call x0 -> x1, Pallas kernels: none -> 27.7 us  [early_exchange(): pl.pallas_call(functools.partial(early_kernel, bits, scan_bits), out_shap...]
    dot_general x3, matrix products: 6.39 us -> 9.57 us  [on_device(): jnp.dot(normed, w_qkv[:, c], preferred_element_type=jnp.float32)]
    pallas_call x2, Pallas kernels: 67.2 us -> 64.6 us  [reduce_scatter(): pl.pallas_call(functools.partial(reduce_kernel, bits, parts), out_shape=j...]
where the time goes in v3:
time: 226 us
  Pallas kernels  149 us (66%)
  matrix products  60.8 us (27%)
  other arithmetic  9.23 us (4%)
  local copies, waits for them, and re-layouts  6.38 us (3%)
    pallas_call x2, Pallas kernels, reduce_scatter(): pl.pallas_call(functools.partial(reduce_kernel, bits, parts), out_shape=j...  64.6 us
    pallas_call x1, Pallas kernels, gather(): pl.pallas_call(functools.partial(gather_kernel, bits, parts), out_shape=j...  56.8 us
    pallas_call x1, Pallas kernels, early_exchange(): pl.pallas_call(functools.partial(early_kernel, bits, scan_bits), out_shap...  27.7 us
    dot_general x1, matrix products, on_device(): jnp.einsum('gjct,jgcd->gtd', picks, rows_out, preferred_element_type=jnp....  13.6 us
    dot_general x1, matrix products, on_device(): jnp.einsum('gjct,gtd->jgcd', picks, everyone, preferred_element_type=jnp....  10.9 us
    dot_general x1, matrix products, on_device(): jnp.einsum('jgcd,jdf->jgcf', rows_in, w_gate_up[:, 0], preferred_element_...  10.1 us
    dot_general x1, matrix products, on_device(): jnp.einsum('jgcd,jdf->jgcf', rows_in, w_gate_up[:, 1], preferred_element_...  9.63 us
    dot_general x3, matrix products, on_device(): jnp.dot(normed, w_qkv[:, c], preferred_element_type=jnp.float32)  9.57 us

profile of v3, /device:TPU:0, one launch (start us, length us, event | category | flops | bytes accessed | tf_op | source)
XLA Modules:
  0.0 225.7 jit_solution(13465063792741893832)
XLA Ops:
  0.0 1.7 multiply_reduce_fusion
  1.7 0.7 convert_element_type.72
  2.4 0.7 maximum_bitcast_fusion
  3.1 3.5 %fusion.56 = bf16[32,4,8,128]{3,2,1,0:T(8,128)(2,1)} fusion(bf16[2048,3,512]{2,0,1:T(8,128)(2,1)} %param.12, f32[2048]{0:T(1024)} %param.11, f32[256]{0:T(256)S(1)} %add_rsqrt_fusion.1, bf16[256,2048]{1,0:T(8,128)(2,1)} %param.10), kind=kOutput, calls=%fused_computation.43 | convolution fusion | flops 539099136 | bytes 3417088 | tf_op jit(solution)/shard_map/dot_general | solution.py:316
  6.6 3.0 %fusion.59 = bf16[32,4,8,128]{3,2,1,0:T(8,128)(2,1)} fusion(bf16[2048,3,512]{2,0,1:T(8,128)(2,1)} %param.12, f32[2048]{0:T(1024)S(1)} %copy-done.8, f32[256]{0:T(256)S(1)} %add_rsqrt_fusion.1, bf16[256,2048]{1,0:T(8,128)(2,1)S(1)} %copy-done.4), kind=kOutput, calls=%fused_computation.44 | convolution fusion | flops 539099136 | bytes 3417088 | tf_op jit(solution)/shard_map/dot_general | solution.py:316
  9.6 3.0 %fusion.44 = bf16[256,512]{1,0:T(8,128)(2,1)} fusion(bf16[2048,3,512]{2,0,1:T(8,128)(2,1)} %param.12, f32[2048]{0:T(1024)S(1)} %copy-done.8, f32[256]{0:T(256)S(1)} %add_rsqrt_fusion.1, bf16[256,2048]{1,0:T(8,128)(2,1)S(1)} %copy-done.4), kind=kOutput, calls=%fused_computation.41 | convolution fusion | flops 539099136 | bytes 3417088 | tf_op jit(solution)/shard_map/dot_general | solution.py:316
  12.7 1.1 copy.66
  13.8 1.3 fusion.74
  15.0 27.7 %early0.1 = (f32[2,2,2,2,2,16,128]{6,5,4,3,2,1,0:T(8,128)S(1)}, f32[512,128]{1,0:T(8,128)S(1)}) custom-call(f32[16,128]{1,0:T(8,128)S(1)} %pad.4.x_ref, f32[512,128]{1,0:T(8,128)S(1)} %bitcast.112), custom_call_target="tpu_custom_call" | custom-call | tf_op jit(solution)/shard_map/early0/pallas_call | solution.py:97
  42.7 0.8 copy.103
  43.5 1.1 reshape.87
  44.6 0.2 fusion.63
  44.8 0.2 compare_reduce_fusion
  45.1 0.3 fusion.67
  45.4 1.1 select_reduce_fusion
  46.5 2.2 fusion.69
  48.7 2.5 %multiply_reduce_fusion.2 = (f32[256,4]{0,1:T(4,128)S(1)}, f32[256,4,128]{0,2,1:T(8,128)}) fusion(f32[4,128,256]{2,1,0:T(8,128)} %fusion.69, bf16[256,4,128]{0,2,1:T(8,128)(2,1)} %bitcast.117, f32[256,256]{1,0:T(8,128)S(1)} %fusion.78, bf16[32,4,8,128]{3,2,1,0:T(8,128)(2,1)} %fusion.56, bf16[32,4,8,128]{3,2,1,0:T(8,128)(2,1)} %fusion.59), kind=kOutput, calls=%fused_computation.57 | convolution fusion | flops 135134208 | bytes 2101248 | tf_op jit(solution)/shard_map/hts,shd->thd/dot_general | solution.py:325
  51.3 1.1 broadcast_multiply_fusion
  52.4 0.1 fusion.65
  52.5 0.7 convolution_convert_fusion
  53.3 10.2 %reduce2.1 = bf16[64,2048]{1,0:T(8,128)(2,1)S(1)} custom-call(bf16[2,2,64,2048]{3,2,1,0:T(8,128)(2,1)S(1)} %bitcast.111), custom_call_target="tpu_custom_call" | custom-call | tf_op jit(solution)/shard_map/reduce2/pallas_call | solution.py:259
  63.5 0.2 convert_element_type.66
  63.7 0.2 multiply_reduce_fusion.1
  63.9 1.1 multiply_convert_fusion.2.x_ref
  65.1 56.8 %gather3.1 = bf16[2,2,2,2,2,64,2048]{6,5,4,3,2,1,0:T(8,128)(2,1)} custom-call(bf16[64,2048]{1,0:T(8,128)(2,1)} %multiply_convert_fusion.2.x_ref), custom_call_target="tpu_custom_call" | custom-call | tf_op jit(solution)/shard_map/gather3/pallas_call | solution.py:177
  121.9 10.9 %convert_bitcast_fusion = bf16[8,4,72,2048]{3,2,0,1:T(8,128)(2,1)} fusion(bf16[4,512,2048,1]{2,1,3,0:T(8,128)(2,1)} %bitcast.115, f32[4,8,512]{2,1,0:T(8,128)S(1)} %fusion.67, pred[4,8,512]{2,1,0:T(8,128)(4,1)S(1)} %bitcast.122), kind=kOutput, calls=%fused_computation.3 | convolution fusion | flops 4838916096 | bytes 17907712 | tf_op jit(solution)/shard_map/gjct,gtd->jgcd/dot_general | solution.py:368
  132.8 10.1 %fusion.4 = f32[8,4,72,256]{3,2,1,0:T(8,128)} fusion(bf16[8,2,2048,256]{3,2,1,0:T(8,128)(2,1)} %param.18, bf16[8,4,72,2048]{3,2,0,1:T(8,128)(2,1)} %convert_bitcast_fusion), kind=kOutput, calls=%fused_computation.6 | convolution fusion | flops 2415919104 | bytes 20185088 | tf_op jit(solution)/shard_map/jgcd,jdf->jgcf/dot_general | solution.py:371
  142.9 9.6 %multiply_convert_fusion = bf16[8,4,72,256]{3,2,1,0:T(8,128)(2,1)S(1)} fusion(f32[8,4,72,256]{3,2,1,0:T(8,128)} %fusion.4, bf16[8,2,2048,256]{3,2,1,0:T(8,128)(2,1)} %param.18, bf16[8,4,72,2048]{3,2,0,1:T(8,128)(2,1)} %convert_bitcast_fusion, f32[8,4,72]{2,1,0:T(4,128)S(1)} %copy.56), kind=kOutput, calls=%fused_computation.18 | convolution fusion | flops 2420047872 | bytes 21373952 | tf_op jit(solution)/shard_map/jgcd,jdf->jgcf/dot_general | solution.py:374
  152.5 13.6 %bitcast_convert_fusion = bf16[4,512,2048]{2,1,0:T(8,128)(2,1)} fusion(f32[4,8,512]{2,1,0:T(8,128)S(1)} %fusion.67, pred[4,8,512]{2,1,0:T(8,128)(4,1)S(1)} %bitcast.123, bf16[8,256,2048]{2,1,0:T(8,128)(2,1)} %param.19, bf16[8,4,72,256]{3,2,1,0:T(8,128)(2,1)S(1)} %multiply_convert_fusion), kind=kOutput, calls=%fused_computation | convolution fusion | flops 7259029504 | bytes 18038784 | tf_op jit(solution)/shard_map/gjct,jgcd->gtd/dot_general | solution.py:382
  166.1 3.4 %copy-done.2 = bf16[4,512,2048]{2,1,0:T(8,128)(2,1)S(1)} copy-done((bf16[4,512,2048]{2,1,0:T(8,128)(2,1)S(1)}, bf16[4,512,2048]{2,1,0:T(8,128)(2,1)}, u32[]{:S(2)}) %copy-start.2) | copy-done | bytes 8388632
  169.5 54.4 %reduce4.1 = bf16[64,2048]{1,0:T(8,128)(2,1)S(1)} custom-call(bf16[2,2,2,2,2,64,2048]{6,5,4,3,2,1,0:T(8,128)(2,1)S(1)} %bitcast.110), custom_call_target="tpu_custom_call" | custom-call | tf_op jit(solution)/shard_map/reduce4/pallas_call | solution.py:259
  223.9 1.8 add_convert_fusion
  (26 shorter events, 0.1 us)
Async XLA Ops:
  0.0 52.5 %copy-start = (bf16[512,2048]{1,0:T(8,128)(2,1)S(1)}, bf16[512,2048]{1,0:T(8,128)(2,1)}, u32[]{:S(2)}) copy-start(bf16[512,2048]{1,0:T(8,128)(2,1)} %param.14) | copy-start | bytes 6291460
  3.1 3.5 %copy-start.4 = (bf16[256,2048]{1,0:T(8,128)(2,1)S(1)}, bf16[256,2048]{1,0:T(8,128)(2,1)}, u32[]{:S(2)}) copy-start(bf16[256,2048]{1,0:T(8,128)(2,1)} %param.10) | copy-start | bytes 3145732
  3.1 3.5 %copy-start.8 = (f32[2048]{0:T(1024)S(1)}, f32[2048]{0:T(1024)}, u32[]{:S(2)}) copy-start(f32[2048]{0:T(1024)} %param.11) | copy-start | bytes 24580
  13.8 1.3 copy-start.5
  45.4 7.0 %copy-start.7 = (f32[512]{0:T(512)S(1)}, f32[512]{0:T(512)}, u32[]{:S(2)}) copy-start(f32[512]{0:T(512)} %param.13) | copy-start | bytes 6148
  53.3 10.7 %copy-start.6 = (f32[2048]{0:T(1024)S(1)}, f32[2048]{0:T(1024)}, u32[]{:S(2)}) copy-start(f32[2048]{0:T(1024)} %param.15) | copy-start | bytes 24580
  63.7 58.2 %copy-start.3 = (f32[256,2048]{1,0:T(8,128)}, f32[256,2048]{1,0:T(8,128)S(1)}, u32[]{:S(2)}) copy-start(f32[256,2048]{1,0:T(8,128)S(1)} %convert_element_type.66) | copy-start | bytes 6291460
  166.1 3.4 %copy-start.2 = (bf16[4,512,2048]{2,1,0:T(8,128)(2,1)S(1)}, bf16[4,512,2048]{2,1,0:T(8,128)(2,1)}, u32[]{:S(2)}) copy-start(bf16[4,512,2048]{2,1,0:T(8,128)(2,1)} %bitcast_convert_fusion) | copy-start | bytes 25165828
  169.5 56.2 %copy-start.1 = (bf16[512,2048]{1,0:T(8,128)(2,1)S(1)}, bf16[512,2048]{1,0:T(8,128)(2,1)}, u32[]{:S(2)}) copy-start(bf16[512,2048]{1,0:T(8,128)(2,1)} %param.14) | copy-start | bytes 6291460
